TPU v7x, 512 devices: a whole 4x8x8 slice. The times are simulated.
512 devices in a mesh: depth: 8 (over y), lat: 32 (over z, x), freq: 2 (over core).
Axes of the slice: x: 4, y: 8, z: 8, core: 2. Of those that a mesh axis runs over, the one named last changes fastest.
Arguments:
- surface: bfloat16 [6, 2, 128, 32768], P('freq', None, None, 'lat'), may hold values from -6 to 6
- refl: float32 [8, 32768], P('depth', 'lat'), may hold values from -0.5 to 0.5
- pool: bfloat16 [8, 6, 8, 128, 256], P('depth', 'freq'), may hold values from -0.375 to 0.375
- tile_ids: int32 [8, 256, 10], P('depth', 'lat'), may hold values from 0 to 255, as said below
- block_ids: int32 [8, 256, 10], P('depth', 'lat'), may hold values from 0 to 7
- counts: int32 [8, 256], P('depth', 'lat'), may hold values from 1 to 10, as said below
Outputs:
- image: float32 [8, 32768], P('depth', 'lat')
Inputs may be any that keep to these rules, and one draw needn't show every extreme that they name: tile_ids[l, j, k] = (j + o) mod 256 for an offset o with -8 <= o <= 8; slot 0 names the row's own tile; in every level some row has all 10 slots live with offsets 8 at slot 1 and -8 at slot 2. Slots k >= counts[l, j] of row j are padding; in every level some row has all 10 slots live.
All inputs are finite; a program needn't handle non-finite values.
Results may differ from a plain program's by a relative error of at most 0.00055.
Values may be sent and summed in bfloat16 or wider, within the bound.
A program may use at most 128 MiB of HBM per device.

v0:
```python
import jax
import jax.numpy as jnp
from jax import lax
from jax.sharding import PartitionSpec as P

TILE = 128
TILE_DEV = 8


def extended_2(block, sides, width):
    for axis, dim in sides:
        count = lax.axis_size(axis)
        forward = [(i, i + 1) for i in range(count - 1)]
        forward.append((count - 1, 0))
        backward = [(target, source) for source, target in forward]
        low = lax.ppermute(
            lax.slice_in_dim(block, block.shape[dim] - width, None, axis=dim), axis, forward
        )
        high = lax.ppermute(lax.slice_in_dim(block, 0, width, axis=dim), axis, backward)
        block = jnp.concatenate([low, block, high], axis=dim)
    return block


def in_one_piece(arrays, axis, dim, along):
    columns = [a.reshape(*a.shape[:along], -1) for a in arrays]
    both = jnp.concatenate(columns, axis=along)
    whole, at, gathered = (lax.all_gather(both, axis, axis=dim, tiled=True), 0, [])
    for a, column in zip(arrays, columns):
        piece = whole[..., at : at + column.shape[along]]
        gathered.append(piece.reshape(*piece.shape[:along], *a.shape[along:]))
        at += column.shape[along]
    return tuple(gathered)


def copy_for_each(shard, axis):
    copies = jnp.broadcast_to(shard, (lax.axis_size(axis), *shard.shape))
    return lax.all_to_all(copies, axis, split_axis=0, concat_axis=0, tiled=True)


def in_order(parts, dim):
    parts = jnp.moveaxis(parts, 0, dim)
    shape = parts.shape
    return parts.reshape(*shape[:dim], shape[dim] * shape[dim + 1], *shape[dim + 2 :])


def gather_directly(shard, axis, dim):
    parts = copy_for_each(shard, axis)
    return in_order(parts, dim)


def cut_along(shard, dim, length):
    before, after = (shard.shape[:dim], shard.shape[dim + 1 :])
    return jnp.moveaxis(shard.reshape(*before, length, -1, *after), dim, 0)


def summed_on_arrival(shard, axis, dim):
    parts = cut_along(shard, dim, lax.axis_size(axis))
    arrived = lax.all_to_all(parts, axis, split_axis=0, concat_axis=0, tiled=True)
    return arrived.sum(axis=0)


def aperture_rim(wave_field):
    return extended_2(wave_field, (("lat", 3),), TILE_DEV * TILE)


def extrapolate(extended, pool_level, local_ids, block_level, count_level, refl_level):
    freqs_here = extended.shape[0]
    shot_rows = extended.shape[2]
    tile_rows = local_ids.shape[0]
    slot_total = local_ids.shape[1]
    tile_grid = extended.reshape(freqs_here, 2, shot_rows, -1, TILE)
    slot_live = (jnp.arange(slot_total)[None, :] < count_level[:, None]).astype(jnp.bfloat16)
    picked = jnp.take(tile_grid, local_ids, axis=3) * slot_live[None, None, None, :, :, None]
    chosen = jnp.take(pool_level, block_level, axis=1)
    product = jnp.einsum("fsarkt,frktc->rfsac", picked, chosen, preferred_element_type=jnp.float32)
    real_part = product[:, :, 0, :, :TILE] - product[:, :, 1, :, TILE:]
    imag_part = product[:, :, 0, :, TILE:] + product[:, :, 1, :, :TILE]
    row_scale = 1.0 / jnp.sqrt(count_level.astype(jnp.float32))
    rows_out = jnp.stack([real_part, imag_part], 2) * row_scale[:, None, None, None, None]
    wave_out = jnp.transpose(rows_out, (1, 2, 3, 0, 4)).reshape(
        freqs_here, 2, shot_rows, tile_rows * TILE
    )
    wave_out = wave_out * (1.0 - refl_level)
    return (wave_out.astype(jnp.bfloat16), jnp.sum(wave_out * wave_out, axis=(0, 1, 2)))


def per_device(surface, refl, pool, tile_ids, block_ids, counts):
    depth_index = lax.axis_index("depth")
    lat_index = lax.axis_index("lat")
    tile_count = TILE_DEV * lax.axis_size("lat")
    first_tile = lat_index * TILE_DEV - TILE_DEV
    freqs_here = surface.shape[0]
    shot_total = surface.shape[2]
    lateral_width = surface.shape[3]
    shot_rows = shot_total // lax.axis_size("depth")
    own_shots = lax.dynamic_slice_in_dim(surface, depth_index * shot_rows, shot_rows, 2)
    pool_all = lax.all_gather(pool, "depth", axis=0, tiled=True)
    ids_all, blocks_all, counts_all = in_one_piece((tile_ids, block_ids, counts), "depth", 0, 2)
    refl_all = gather_directly(refl, "depth", 0)
    level_total = pool_all.shape[0]

    def level_step(level_index, loop_state):
        wave_field, images = loop_state
        ids_here = lax.dynamic_index_in_dim(ids_all, level_index, 0, keepdims=False)
        local_level = jnp.mod(ids_here - first_tile, tile_count)
        pool_here = lax.dynamic_index_in_dim(pool_all, level_index, 0, keepdims=False)
        blocks_here = lax.dynamic_index_in_dim(blocks_all, level_index, 0, keepdims=False)
        counts_here = lax.dynamic_index_in_dim(counts_all, level_index, 0, keepdims=False)
        refl_here = lax.dynamic_index_in_dim(refl_all, level_index, 0, keepdims=False)
        handed, partial_value = extrapolate(
            aperture_rim(wave_field), pool_here, local_level, blocks_here, counts_here, refl_here
        )
        images = lax.dynamic_update_index_in_dim(images, partial_value, level_index, 0)
        return (handed, images)

    start_images = jnp.zeros((level_total, lateral_width), jnp.float32)
    loop_state = lax.fori_loop(0, level_total, level_step, (own_shots, start_images))
    image_local = summed_on_arrival(loop_state[1], "depth", 0)[0]
    summed = lax.psum(image_local, "freq")
    divisor = freqs_here * lax.axis_size("freq") * shot_total
    return (summed / divisor)[None, :]


def solution(mesh):
    placed = (
        P("freq", None, None, "lat"),
        P("depth", "lat"),
        P("depth", "freq", None, None, None),
        P("depth", "lat", None),
        P("depth", "lat", None),
        P("depth", "lat"),
    )
    return jax.shard_map(
        per_device, mesh=mesh, in_specs=placed, out_specs=P("depth", "lat"), check_vma=False
    )
```

profile of v0, /device:TPU:1, one launch (start us, length us, event | category | flops | bytes accessed | tf_op | source)
XLA Modules:
  0.0 460.4 jit_solution(3497054629939524282)
XLA Ops:
  8.6 7.7 %all-to-all-start = ((f32[8,1,1024]{2,1,0:T(1,128)}), f32[8,1,1024]{2,1,0:T(1,128)S(1)}, u32[]{:S(2)}, u32[]{:S(2)}) async-start(f32[8,1,1024]{2,1,0:T(1,128)} %broadcast_in_dim.88), calls=%async_computation | async-start | bytes 65536 | tf_op jit(solution)/shard_map/all_to_all | solution.py:37
  17.7 20.8 %all_gather.6 = s32[8,8,21]{2,1,0:T(8,128)S(1)} all-gather(s32[1,8,21]{2,1,0:T(8,128)S(1)} %pad_add_fusion), channel_id=1, replica_groups=mesh['depth'=8,'lat'=32,'freq'=2] {'depth'}, dimensions={0}, use_global_device_ids=true | all-gather | bytes 6048 | tf_op jit(solution)/shard_map/all_gather | solution.py:27
  40.0 110.9 %all-gather.2.cloned.1.call-done = bf16[8,3,8,128,256]{4,3,2,1,0:T(8,128)(2,1)} async-done(((bf16[1,3,8,128,256]{4,3,2,1,0:T(8,128)(2,1)}), bf16[8,3,8,128,256]{4,3,2,1,0:T(8,128)(2,1)}) %all-gather.2.cloned.1.call-update) | async-done | bytes 12582928 | tf_op jit(solution)/shard_map/all_gather | solution.py:97
  150.9 281.9 %while.17 = (s32[]{:T(128)}, bf16[3,2,16,1024]{3,2,1,0:T(8,128)(2,1)S(1)}, f32[8,1024]{1,0:T(8,128)}, s32[8,8,10]{2,1,0:T(8,128)S(1)}, s32[]{:T(128)}, /*index=5...) while((s32[]{:T(128)}, ...), condition=%wide.region_2.3_spmd, body=%wide.region_0.2_spmd.sunk | while | flops 515904960 | bytes 62015692 | solution.py:117
  150.9 7.8 %collective-permute-start = (bf16[3,2,16,1024]{3,2,1,0:T(8,128)(2,1)S(1)}, bf16[3,2,16,1024]{3,2,1,0:T(8,128)(2,1)S(1)}, u32[]{:S(2)}, u32[]{:S(2)}) collective-permute-start(bf16[3,2,16,1024]{3,2,1,0:T(8,128)(2,1)S(1)} %get-tuple-element.365), channel_id=1, source_target_pairs={{2,0},{4,2},{6,4},{8,6},{10,8},{12,10},{14,12},{16,14},{18,16},{20... | collective-permute-start | bytes 589832 | tf_op jit(solution)/shard_map/while/body/eval_jaxpr/ppermute | solution.py:19
  164.9 8.1 %gather_fusion = bf16[80,3,128,256]{3,2,1,0:T(8,128)(2,1)} fusion(bf16[3,8,128,256]{3,2,1,0:T(8,128)(2,1)S(1)} %dynamic-slice_bitcast_fusion.2, s32[1024]{0:T(1024)S(1)} %pad_clamp_fusion.4), kind=kCustom, calls=%fused_computation.1.clone.1 | custom fusion | bytes 31457600 | tf_op jit(solution)/shard_map/while/body/eval_jaxpr/jit(_take)/gather | solution.py:74
  177.3 8.0 %fusion.30 = f32[8,3,2,16,256]{4,3,2,1,0:T(8,128)S(1)} fusion(bf16[8,10,3,128,256]{4,3,2,1,0:T(8,128)(2,1)} %bitcast.98, pred[8,10]{1,0:T(8,128)(4,1)S(1)} %copy-done.5, bf16[8,10,3,2,16,128]{5,4,3,2,1,0:T(8,128)(2,1)} %bitcast.99, pred[8,10]{1,0:T(8,128)(4,1)S(1)} %copy-done.6, bf16[8,10]{1,0:T(8,128)(2,1)S(1)} %fusion.29), kind=kOutput, calls=%fused_computation.8.clone.1 | convolution fusion | flops 513146880 | bytes 18481472 | tf_op jit(solution)/shard_map/while/body/eval_jaxpr/fsarkt,frktc->rfsac/dot_general | solution.py:75
  200.1 8.2 %gather_fusion = bf16[80,3,128,256]{3,2,1,0:T(8,128)(2,1)} fusion(bf16[3,8,128,256]{3,2,1,0:T(8,128)(2,1)S(1)} %dynamic-slice_bitcast_fusion.2, s32[1024]{0:T(1024)S(1)} %pad_clamp_fusion.4), kind=kCustom, calls=%fused_computation.1.clone.1 | custom fusion | bytes 31457600 | tf_op jit(solution)/shard_map/while/body/eval_jaxpr/jit(_take)/gather | solution.py:74
  212.4 8.0 %fusion.30 = f32[8,3,2,16,256]{4,3,2,1,0:T(8,128)S(1)} fusion(bf16[8,10,3,128,256]{4,3,2,1,0:T(8,128)(2,1)} %bitcast.98, pred[8,10]{1,0:T(8,128)(4,1)S(1)} %copy-done.5, bf16[8,10,3,2,16,128]{5,4,3,2,1,0:T(8,128)(2,1)} %bitcast.99, pred[8,10]{1,0:T(8,128)(4,1)S(1)} %copy-done.6, bf16[8,10]{1,0:T(8,128)(2,1)S(1)} %fusion.29), kind=kOutput, calls=%fused_computation.8.clone.1 | convolution fusion | flops 513146880 | bytes 18481472 | tf_op jit(solution)/shard_map/while/body/eval_jaxpr/fsarkt,frktc->rfsac/dot_general | solution.py:75
  235.1 8.1 %gather_fusion = bf16[80,3,128,256]{3,2,1,0:T(8,128)(2,1)} fusion(bf16[3,8,128,256]{3,2,1,0:T(8,128)(2,1)S(1)} %dynamic-slice_bitcast_fusion.2, s32[1024]{0:T(1024)S(1)} %pad_clamp_fusion.4), kind=kCustom, calls=%fused_computation.1.clone.1 | custom fusion | bytes 31457600 | tf_op jit(solution)/shard_map/while/body/eval_jaxpr/jit(_take)/gather | solution.py:74
  247.5 8.0 %fusion.30 = f32[8,3,2,16,256]{4,3,2,1,0:T(8,128)S(1)} fusion(bf16[8,10,3,128,256]{4,3,2,1,0:T(8,128)(2,1)} %bitcast.98, pred[8,10]{1,0:T(8,128)(4,1)S(1)} %copy-done.5, bf16[8,10,3,2,16,128]{5,4,3,2,1,0:T(8,128)(2,1)} %bitcast.99, pred[8,10]{1,0:T(8,128)(4,1)S(1)} %copy-done.6, bf16[8,10]{1,0:T(8,128)(2,1)S(1)} %fusion.29), kind=kOutput, calls=%fused_computation.8.clone.1 | convolution fusion | flops 513146880 | bytes 18481472 | tf_op jit(solution)/shard_map/while/body/eval_jaxpr/fsarkt,frktc->rfsac/dot_general | solution.py:75
  257.3 6.7 %collective-permute-start = (bf16[3,2,16,1024]{3,2,1,0:T(8,128)(2,1)S(1)}, bf16[3,2,16,1024]{3,2,1,0:T(8,128)(2,1)S(1)}, u32[]{:S(2)}, u32[]{:S(2)}) collective-permute-start(bf16[3,2,16,1024]{3,2,1,0:T(8,128)(2,1)S(1)} %get-tuple-element.365), channel_id=1, source_target_pairs={{2,0},{4,2},{6,4},{8,6},{10,8},{12,10},{14,12},{16,14},{18,16},{20... | collective-permute-start | bytes 589832 | tf_op jit(solution)/shard_map/while/body/eval_jaxpr/ppermute | solution.py:19
  270.3 8.2 %gather_fusion = bf16[80,3,128,256]{3,2,1,0:T(8,128)(2,1)} fusion(bf16[3,8,128,256]{3,2,1,0:T(8,128)(2,1)S(1)} %dynamic-slice_bitcast_fusion.2, s32[1024]{0:T(1024)S(1)} %pad_clamp_fusion.4), kind=kCustom, calls=%fused_computation.1.clone.1 | custom fusion | bytes 31457600 | tf_op jit(solution)/shard_map/while/body/eval_jaxpr/jit(_take)/gather | solution.py:74
  282.7 8.0 %fusion.30 = f32[8,3,2,16,256]{4,3,2,1,0:T(8,128)S(1)} fusion(bf16[8,10,3,128,256]{4,3,2,1,0:T(8,128)(2,1)} %bitcast.98, pred[8,10]{1,0:T(8,128)(4,1)S(1)} %copy-done.5, bf16[8,10,3,2,16,128]{5,4,3,2,1,0:T(8,128)(2,1)} %bitcast.99, pred[8,10]{1,0:T(8,128)(4,1)S(1)} %copy-done.6, bf16[8,10]{1,0:T(8,128)(2,1)S(1)} %fusion.29), kind=kOutput, calls=%fused_computation.8.clone.1 | convolution fusion | flops 513146880 | bytes 18481472 | tf_op jit(solution)/shard_map/while/body/eval_jaxpr/fsarkt,frktc->rfsac/dot_general | solution.py:75
  305.4 8.1 %gather_fusion = bf16[80,3,128,256]{3,2,1,0:T(8,128)(2,1)} fusion(bf16[3,8,128,256]{3,2,1,0:T(8,128)(2,1)S(1)} %dynamic-slice_bitcast_fusion.2, s32[1024]{0:T(1024)S(1)} %pad_clamp_fusion.4), kind=kCustom, calls=%fused_computation.1.clone.1 | custom fusion | bytes 31457600 | tf_op jit(solution)/shard_map/while/body/eval_jaxpr/jit(_take)/gather | solution.py:74
  317.7 8.0 %fusion.30 = f32[8,3,2,16,256]{4,3,2,1,0:T(8,128)S(1)} fusion(bf16[8,10,3,128,256]{4,3,2,1,0:T(8,128)(2,1)} %bitcast.98, pred[8,10]{1,0:T(8,128)(4,1)S(1)} %copy-done.5, bf16[8,10,3,2,16,128]{5,4,3,2,1,0:T(8,128)(2,1)} %bitcast.99, pred[8,10]{1,0:T(8,128)(4,1)S(1)} %copy-done.6, bf16[8,10]{1,0:T(8,128)(2,1)S(1)} %fusion.29), kind=kOutput, calls=%fused_computation.8.clone.1 | convolution fusion | flops 513146880 | bytes 18481472 | tf_op jit(solution)/shard_map/while/body/eval_jaxpr/fsarkt,frktc->rfsac/dot_general | solution.py:75
  340.5 8.2 %gather_fusion = bf16[80,3,128,256]{3,2,1,0:T(8,128)(2,1)} fusion(bf16[3,8,128,256]{3,2,1,0:T(8,128)(2,1)S(1)} %dynamic-slice_bitcast_fusion.2, s32[1024]{0:T(1024)S(1)} %pad_clamp_fusion.4), kind=kCustom, calls=%fused_computation.1.clone.1 | custom fusion | bytes 31457600 | tf_op jit(solution)/shard_map/while/body/eval_jaxpr/jit(_take)/gather | solution.py:74
  352.9 8.0 %fusion.30 = f32[8,3,2,16,256]{4,3,2,1,0:T(8,128)S(1)} fusion(bf16[8,10,3,128,256]{4,3,2,1,0:T(8,128)(2,1)} %bitcast.98, pred[8,10]{1,0:T(8,128)(4,1)S(1)} %copy-done.5, bf16[8,10,3,2,16,128]{5,4,3,2,1,0:T(8,128)(2,1)} %bitcast.99, pred[8,10]{1,0:T(8,128)(4,1)S(1)} %copy-done.6, bf16[8,10]{1,0:T(8,128)(2,1)S(1)} %fusion.29), kind=kOutput, calls=%fused_computation.8.clone.1 | convolution fusion | flops 513146880 | bytes 18481472 | tf_op jit(solution)/shard_map/while/body/eval_jaxpr/fsarkt,frktc->rfsac/dot_general | solution.py:75
  375.6 8.2 %gather_fusion = bf16[80,3,128,256]{3,2,1,0:T(8,128)(2,1)} fusion(bf16[3,8,128,256]{3,2,1,0:T(8,128)(2,1)S(1)} %dynamic-slice_bitcast_fusion.2, s32[1024]{0:T(1024)S(1)} %pad_clamp_fusion.4), kind=kCustom, calls=%fused_computation.1.clone.1 | custom fusion | bytes 31457600 | tf_op jit(solution)/shard_map/while/body/eval_jaxpr/jit(_take)/gather | solution.py:74
  387.9 8.0 %fusion.30 = f32[8,3,2,16,256]{4,3,2,1,0:T(8,128)S(1)} fusion(bf16[8,10,3,128,256]{4,3,2,1,0:T(8,128)(2,1)} %bitcast.98, pred[8,10]{1,0:T(8,128)(4,1)S(1)} %copy-done.5, bf16[8,10,3,2,16,128]{5,4,3,2,1,0:T(8,128)(2,1)} %bitcast.99, pred[8,10]{1,0:T(8,128)(4,1)S(1)} %copy-done.6, bf16[8,10]{1,0:T(8,128)(2,1)S(1)} %fusion.29), kind=kOutput, calls=%fused_computation.8.clone.1 | convolution fusion | flops 513146880 | bytes 18481472 | tf_op jit(solution)/shard_map/while/body/eval_jaxpr/fsarkt,frktc->rfsac/dot_general | solution.py:75
  410.7 8.2 %gather_fusion = bf16[80,3,128,256]{3,2,1,0:T(8,128)(2,1)} fusion(bf16[3,8,128,256]{3,2,1,0:T(8,128)(2,1)S(1)} %dynamic-slice_bitcast_fusion.2, s32[1024]{0:T(1024)S(1)} %pad_clamp_fusion.4), kind=kCustom, calls=%fused_computation.1.clone.1 | custom fusion | bytes 31457600 | tf_op jit(solution)/shard_map/while/body/eval_jaxpr/jit(_take)/gather | solution.py:74
  423.0 8.0 %fusion.30 = f32[8,3,2,16,256]{4,3,2,1,0:T(8,128)S(1)} fusion(bf16[8,10,3,128,256]{4,3,2,1,0:T(8,128)(2,1)} %bitcast.98, pred[8,10]{1,0:T(8,128)(4,1)S(1)} %copy-done.5, bf16[8,10,3,2,16,128]{5,4,3,2,1,0:T(8,128)(2,1)} %bitcast.99, pred[8,10]{1,0:T(8,128)(4,1)S(1)} %copy-done.6, bf16[8,10]{1,0:T(8,128)(2,1)S(1)} %fusion.29), kind=kOutput, calls=%fused_computation.8.clone.1 | convolution fusion | flops 513146880 | bytes 18481472 | tf_op jit(solution)/shard_map/while/body/eval_jaxpr/fsarkt,frktc->rfsac/dot_general | solution.py:75
  433.6 10.9 %all_to_all.10 = f32[8,1,1024]{2,1,0:T(1,128)S(1)} all-to-all(f32[8,1,1024]{2,1,0:T(1,128)S(1)} %reshape.218), channel_id=1, replica_groups=mesh['depth'=8,'lat'=32,'freq'=2] {'depth'}, dimensions={0} | all-to-all | bytes 65536 | tf_op jit(solution)/shard_map/all_to_all | solution.py:58
  444.5 8.4 %psum.7 = f32[1024]{0:T(1024)S(1)} all-reduce(f32[1024]{0:T(1024)S(1)} %reduce_sum.20), channel_id=1, replica_groups=mesh['depth'=8,'lat'=32,'freq'=2] {'freq'}, use_global_device_ids=true, to_apply=%region_4.5 | all-reduce | flops 1024 | bytes 8192 | tf_op jit(solution)/shard_map/psum | solution.py:119
  (271 shorter events, 143.4 us)
Async XLA Ops:
  6.5 32.0 %copy-start = (bf16[3,2,128,1024]{3,2,1,0:T(8,128)(2,1)S(1)}, bf16[3,2,128,1024]{3,2,1,0:T(8,128)(2,1)}, u32[]{:S(2)}) copy-start(bf16[3,2,128,1024]{3,2,1,0:T(8,128)(2,1)} %param.8) | copy-start | bytes 4718596
  6.5 144.3 %all-gather.2.cloned.1.call-start = ((), (), s32[]{:S(2)}) async-start(), calls=%async_computation.2 | async-start | bytes 14155776 | tf_op jit(solution)/shard_map/all_gather | solution.py:97
  8.6 30.8 %all-to-all-start = ((f32[8,1,1024]{2,1,0:T(1,128)}), f32[8,1,1024]{2,1,0:T(1,128)S(1)}, u32[]{:S(2)}, u32[]{:S(2)}) async-start(f32[8,1,1024]{2,1,0:T(1,128)} %broadcast_in_dim.88), calls=%async_computation | async-start | bytes 65536 | tf_op jit(solution)/shard_map/all_to_all | solution.py:37
  150.9 10.4 %copy-start.1 = (s32[8,8,10]{2,1,0:T(8,128)}, s32[8,8,10]{2,1,0:T(8,128)S(1)}, u32[]{:S(2)}) copy-start(s32[8,8,10]{2,1,0:T(8,128)S(1)} %get-tuple-element.381) | copy-start | bytes 7684 | tf_op jit(solution)/shard_map/while
  150.9 10.4 %copy-start.3 = (s32[8,8,10]{2,1,0:T(8,128)}, s32[8,8,10]{2,1,0:T(8,128)S(1)}, u32[]{:S(2)}) copy-start(s32[8,8,10]{2,1,0:T(8,128)S(1)} %get-tuple-element.378) | copy-start | bytes 7684 | tf_op jit(solution)/shard_map/while
  150.9 22.9 %collective-permute-start = (bf16[3,2,16,1024]{3,2,1,0:T(8,128)(2,1)S(1)}, bf16[3,2,16,1024]{3,2,1,0:T(8,128)(2,1)S(1)}, u32[]{:S(2)}, u32[]{:S(2)}) collective-permute-start(bf16[3,2,16,1024]{3,2,1,0:T(8,128)(2,1)S(1)} %get-tuple-element.365), channel_id=1, source_target_pairs={{2,0},{4,2},{6,4},{8,6},{10,8},{12,10},{14,12},{16,14},{18,16},{20... | collective-permute-start | bytes 589832 | tf_op jit(solution)/shard_map/while/body/eval_jaxpr/ppermute | solution.py:19
  158.7 15.1 %collective-permute-start.1 = (bf16[3,2,16,1024]{3,2,1,0:T(8,128)(2,1)S(1)}, bf16[3,2,16,1024]{3,2,1,0:T(8,128)(2,1)}, u32[]{:S(2)}, u32[]{:S(2)}) collective-permute-start(bf16[3,2,16,1024]{3,2,1,0:T(8,128)(2,1)S(1)} %get-tuple-element.365), channel_id=1, source_target_pairs={{0,2},{2,4},{4,6},{6,8},{8,10},{10,12},{12,14},{14,16},{16,18},{18... | collective-permute-start | bytes 589832 | tf_op jit(solution)/shard_map/while/body/eval_jaxpr/ppermute | solution.py:16
  187.0 9.4 %copy-start.3 = (s32[8,8,10]{2,1,0:T(8,128)}, s32[8,8,10]{2,1,0:T(8,128)S(1)}, u32[]{:S(2)}) copy-start(s32[8,8,10]{2,1,0:T(8,128)S(1)} %get-tuple-element.378) | copy-start | bytes 7684 | tf_op jit(solution)/shard_map/while
  187.1 21.9 %collective-permute-start = (bf16[3,2,16,1024]{3,2,1,0:T(8,128)(2,1)S(1)}, bf16[3,2,16,1024]{3,2,1,0:T(8,128)(2,1)S(1)}, u32[]{:S(2)}, u32[]{:S(2)}) collective-permute-start(bf16[3,2,16,1024]{3,2,1,0:T(8,128)(2,1)S(1)} %get-tuple-element.365), channel_id=1, source_target_pairs={{2,0},{4,2},{6,4},{8,6},{10,8},{12,10},{14,12},{16,14},{18,16},{20... | collective-permute-start | bytes 589832 | tf_op jit(solution)/shard_map/while/body/eval_jaxpr/ppermute | solution.py:19
  193.8 15.2 %collective-permute-start.1 = (bf16[3,2,16,1024]{3,2,1,0:T(8,128)(2,1)S(1)}, bf16[3,2,16,1024]{3,2,1,0:T(8,128)(2,1)}, u32[]{:S(2)}, u32[]{:S(2)}) collective-permute-start(bf16[3,2,16,1024]{3,2,1,0:T(8,128)(2,1)S(1)} %get-tuple-element.365), channel_id=1, source_target_pairs={{0,2},{2,4},{4,6},{6,8},{8,10},{10,12},{12,14},{14,16},{16,18},{18... | collective-permute-start | bytes 589832 | tf_op jit(solution)/shard_map/while/body/eval_jaxpr/ppermute | solution.py:16
  222.2 21.8 %collective-permute-start = (bf16[3,2,16,1024]{3,2,1,0:T(8,128)(2,1)S(1)}, bf16[3,2,16,1024]{3,2,1,0:T(8,128)(2,1)S(1)}, u32[]{:S(2)}, u32[]{:S(2)}) collective-permute-start(bf16[3,2,16,1024]{3,2,1,0:T(8,128)(2,1)S(1)} %get-tuple-element.365), channel_id=1, source_target_pairs={{2,0},{4,2},{6,4},{8,6},{10,8},{12,10},{14,12},{16,14},{18,16},{20... | collective-permute-start | bytes 589832 | tf_op jit(solution)/shard_map/while/body/eval_jaxpr/ppermute | solution.py:19
  228.9 15.1 %collective-permute-start.1 = (bf16[3,2,16,1024]{3,2,1,0:T(8,128)(2,1)S(1)}, bf16[3,2,16,1024]{3,2,1,0:T(8,128)(2,1)}, u32[]{:S(2)}, u32[]{:S(2)}) collective-permute-start(bf16[3,2,16,1024]{3,2,1,0:T(8,128)(2,1)S(1)} %get-tuple-element.365), channel_id=1, source_target_pairs={{0,2},{2,4},{4,6},{6,8},{8,10},{10,12},{12,14},{14,16},{16,18},{18... | collective-permute-start | bytes 589832 | tf_op jit(solution)/shard_map/while/body/eval_jaxpr/ppermute | solution.py:16
  257.3 9.4 %copy-start.1 = (s32[8,8,10]{2,1,0:T(8,128)}, s32[8,8,10]{2,1,0:T(8,128)S(1)}, u32[]{:S(2)}) copy-start(s32[8,8,10]{2,1,0:T(8,128)S(1)} %get-tuple-element.381) | copy-start | bytes 7684 | tf_op jit(solution)/shard_map/while
  257.3 9.4 %copy-start.3 = (s32[8,8,10]{2,1,0:T(8,128)}, s32[8,8,10]{2,1,0:T(8,128)S(1)}, u32[]{:S(2)}) copy-start(s32[8,8,10]{2,1,0:T(8,128)S(1)} %get-tuple-element.378) | copy-start | bytes 7684 | tf_op jit(solution)/shard_map/while
  257.3 21.9 %collective-permute-start = (bf16[3,2,16,1024]{3,2,1,0:T(8,128)(2,1)S(1)}, bf16[3,2,16,1024]{3,2,1,0:T(8,128)(2,1)S(1)}, u32[]{:S(2)}, u32[]{:S(2)}) collective-permute-start(bf16[3,2,16,1024]{3,2,1,0:T(8,128)(2,1)S(1)} %get-tuple-element.365), channel_id=1, source_target_pairs={{2,0},{4,2},{6,4},{8,6},{10,8},{12,10},{14,12},{16,14},{18,16},{20... | collective-permute-start | bytes 589832 | tf_op jit(solution)/shard_map/while/body/eval_jaxpr/ppermute | solution.py:19
  264.0 15.2 %collective-permute-start.1 = (bf16[3,2,16,1024]{3,2,1,0:T(8,128)(2,1)S(1)}, bf16[3,2,16,1024]{3,2,1,0:T(8,128)(2,1)}, u32[]{:S(2)}, u32[]{:S(2)}) collective-permute-start(bf16[3,2,16,1024]{3,2,1,0:T(8,128)(2,1)S(1)} %get-tuple-element.365), channel_id=1, source_target_pairs={{0,2},{2,4},{4,6},{6,8},{8,10},{10,12},{12,14},{14,16},{16,18},{18... | collective-permute-start | bytes 589832 | tf_op jit(solution)/shard_map/while/body/eval_jaxpr/ppermute | solution.py:16
  292.4 21.8 %collective-permute-start = (bf16[3,2,16,1024]{3,2,1,0:T(8,128)(2,1)S(1)}, bf16[3,2,16,1024]{3,2,1,0:T(8,128)(2,1)S(1)}, u32[]{:S(2)}, u32[]{:S(2)}) collective-permute-start(bf16[3,2,16,1024]{3,2,1,0:T(8,128)(2,1)S(1)} %get-tuple-element.365), channel_id=1, source_target_pairs={{2,0},{4,2},{6,4},{8,6},{10,8},{12,10},{14,12},{16,14},{18,16},{20... | collective-permute-start | bytes 589832 | tf_op jit(solution)/shard_map/while/body/eval_jaxpr/ppermute | solution.py:19
  299.1 15.1 %collective-permute-start.1 = (bf16[3,2,16,1024]{3,2,1,0:T(8,128)(2,1)S(1)}, bf16[3,2,16,1024]{3,2,1,0:T(8,128)(2,1)}, u32[]{:S(2)}, u32[]{:S(2)}) collective-permute-start(bf16[3,2,16,1024]{3,2,1,0:T(8,128)(2,1)S(1)} %get-tuple-element.365), channel_id=1, source_target_pairs={{0,2},{2,4},{4,6},{6,8},{8,10},{10,12},{12,14},{14,16},{16,18},{18... | collective-permute-start | bytes 589832 | tf_op jit(solution)/shard_map/while/body/eval_jaxpr/ppermute | solution.py:16
  327.5 21.9 %collective-permute-start = (bf16[3,2,16,1024]{3,2,1,0:T(8,128)(2,1)S(1)}, bf16[3,2,16,1024]{3,2,1,0:T(8,128)(2,1)S(1)}, u32[]{:S(2)}, u32[]{:S(2)}) collective-permute-start(bf16[3,2,16,1024]{3,2,1,0:T(8,128)(2,1)S(1)} %get-tuple-element.365), channel_id=1, source_target_pairs={{2,0},{4,2},{6,4},{8,6},{10,8},{12,10},{14,12},{16,14},{18,16},{20... | collective-permute-start | bytes 589832 | tf_op jit(solution)/shard_map/while/body/eval_jaxpr/ppermute | solution.py:19
  334.2 15.2 %collective-permute-start.1 = (bf16[3,2,16,1024]{3,2,1,0:T(8,128)(2,1)S(1)}, bf16[3,2,16,1024]{3,2,1,0:T(8,128)(2,1)}, u32[]{:S(2)}, u32[]{:S(2)}) collective-permute-start(bf16[3,2,16,1024]{3,2,1,0:T(8,128)(2,1)S(1)} %get-tuple-element.365), channel_id=1, source_target_pairs={{0,2},{2,4},{4,6},{6,8},{8,10},{10,12},{12,14},{14,16},{16,18},{18... | collective-permute-start | bytes 589832 | tf_op jit(solution)/shard_map/while/body/eval_jaxpr/ppermute | solution.py:16
  362.7 21.8 %collective-permute-start = (bf16[3,2,16,1024]{3,2,1,0:T(8,128)(2,1)S(1)}, bf16[3,2,16,1024]{3,2,1,0:T(8,128)(2,1)S(1)}, u32[]{:S(2)}, u32[]{:S(2)}) collective-permute-start(bf16[3,2,16,1024]{3,2,1,0:T(8,128)(2,1)S(1)} %get-tuple-element.365), channel_id=1, source_target_pairs={{2,0},{4,2},{6,4},{8,6},{10,8},{12,10},{14,12},{16,14},{18,16},{20... | collective-permute-start | bytes 589832 | tf_op jit(solution)/shard_map/while/body/eval_jaxpr/ppermute | solution.py:19
  369.3 15.2 %collective-permute-start.1 = (bf16[3,2,16,1024]{3,2,1,0:T(8,128)(2,1)S(1)}, bf16[3,2,16,1024]{3,2,1,0:T(8,128)(2,1)}, u32[]{:S(2)}, u32[]{:S(2)}) collective-permute-start(bf16[3,2,16,1024]{3,2,1,0:T(8,128)(2,1)S(1)} %get-tuple-element.365), channel_id=1, source_target_pairs={{0,2},{2,4},{4,6},{6,8},{8,10},{10,12},{12,14},{14,16},{16,18},{18... | collective-permute-start | bytes 589832 | tf_op jit(solution)/shard_map/while/body/eval_jaxpr/ppermute | solution.py:16
  397.7 21.8 %collective-permute-start = (bf16[3,2,16,1024]{3,2,1,0:T(8,128)(2,1)S(1)}, bf16[3,2,16,1024]{3,2,1,0:T(8,128)(2,1)S(1)}, u32[]{:S(2)}, u32[]{:S(2)}) collective-permute-start(bf16[3,2,16,1024]{3,2,1,0:T(8,128)(2,1)S(1)} %get-tuple-element.365), channel_id=1, source_target_pairs={{2,0},{4,2},{6,4},{8,6},{10,8},{12,10},{14,12},{16,14},{18,16},{20... | collective-permute-start | bytes 589832 | tf_op jit(solution)/shard_map/while/body/eval_jaxpr/ppermute | solution.py:19
  404.4 15.1 %collective-permute-start.1 = (bf16[3,2,16,1024]{3,2,1,0:T(8,128)(2,1)S(1)}, bf16[3,2,16,1024]{3,2,1,0:T(8,128)(2,1)}, u32[]{:S(2)}, u32[]{:S(2)}) collective-permute-start(bf16[3,2,16,1024]{3,2,1,0:T(8,128)(2,1)S(1)} %get-tuple-element.365), channel_id=1, source_target_pairs={{0,2},{2,4},{4,6},{6,8},{8,10},{10,12},{12,14},{14,16},{16,18},{18... | collective-permute-start | bytes 589832 | tf_op jit(solution)/shard_map/while/body/eval_jaxpr/ppermute | solution.py:16
  (43 other events, 169.2 us)
Sparse Core Ops, SparseCore 0:
  9.4 141.3 all-gather.1
where the time goes:
time: 463 us; the launch traced here: 460 us
  local copies, waits for them, and re-layouts  114 us (25%)
  waiting for transfers between devices  112 us (24%)
  starting transfers between devices  77.6 us (17%)
  matrix products  64.4 us (14%)
  blocking collectives  40.1 us (9%)
  other arithmetic  38.8 us (8%)
  between operations  13.4 us (3%)
    all_gather x1, waiting for transfers between devices, per_device(): pool_all = lax.all_gather(pool, 'depth', axis=0, tiled=True)  111 us
    gather x8, local copies, waits for them, and re-layouts, extrapolate(): chosen = jnp.take(pool_level, block_level, axis=1)  65.3 us
    dot_general x8, matrix products, extrapolate(): jnp.einsum('fsarkt,frktc->rfsac', picked, chosen, preferred_element_type=...  64.4 us
    ppermute x8, starting transfers between devices, extended_2(): lax.ppermute(lax.slice_in_dim(block, 0, width, axis=dim), axis, backward)  54.6 us
    all_gather x1, blocking collectives, in_one_piece(): lax.all_gather(both, axis, axis=dim, tiled=True)  20.8 us
    gather x8, local copies, waits for them, and re-layouts, extrapolate(): jnp.take(tile_grid, local_ids, axis=3)  19.3 us
    ppermute x8, starting transfers between devices, extended_2(): lax.ppermute(lax.slice_in_dim(block, block.shape[dim] - width, None, axis...  15.4 us
    squeeze x8, local copies, waits for them, and re-layouts, level_step(): lax.dynamic_index_in_dim(pool_all, level_index, 0, keepdims=False)  12.1 us
  transfers between devices with their start and end apart: 18, of which 1 were waited for; matrix products, arithmetic and copies ran while one was open for 24% of the time, Pallas kernels for 0%

commit v1 on v0

--- a/solution.py
+++ b/solution.py
@@ -94,7 +94,9 @@
     lateral_width = surface.shape[3]
     shot_rows = shot_total // lax.axis_size("depth")
     own_shots = lax.dynamic_slice_in_dim(surface, depth_index * shot_rows, shot_rows, 2)
-    pool_all = lax.all_gather(pool, "depth", axis=0, tiled=True)
+    pool_all = jnp.concatenate(
+        lax.all_to_all(jnp.stack([pool] * lax.axis_size("depth")), "depth", 0, 0), axis=0
+    )
     ids_all, blocks_all, counts_all = in_one_piece((tile_ids, block_ids, counts), "depth", 0, 2)
     refl_all = gather_directly(refl, "depth", 0)
     level_total = pool_all.shape[0]

time: 463 us -> 633 us (1.37)
  blocking collectives: 40.1 us -> 326 us
  waiting for transfers between devices: 112 us -> 0.04 us
  between operations: 13.4 us -> 0.05 us
    all_gather x1, blocking collectives: 20.8 us -> 286 us  [in_one_piece(): lax.all_gather(both, axis, axis=dim, tiled=True)]
    all_gather x1 -> x0, waiting for transfers between devices: 111 us -> none  [per_device(): pool_all = lax.all_gather(pool, 'depth', axis=0, tiled=True)]
    all_to_all x0 -> x1, blocking collectives: none -> 14.3 us  [copy_for_each(): return lax.all_to_all(copies, axis, split_axis=0, concat_axis=0, tiled=True)]
    another operation x0 -> x1, local copies, waits for them, and re-layouts: none -> 7.53 us  [per_device(): jnp.stack([pool] * lax.axis_size('depth'))]
  transfers between devices with their start and end apart: 18 -> 17, of which waited for: 1 -> 0; matrix products, arithmetic and copies ran while one was open for 24% -> 17% of each run, Pallas kernels for 0% -> 0%
where the time goes in v1:
time: 633 us; the launch traced here: 630 us
  blocking collectives  326 us (52%)
  local copies, waits for them, and re-layouts  120 us (19%)
  starting transfers between devices  80.5 us (13%)
  matrix products  64.4 us (10%)
  other arithmetic  38.1 us (6%)
    all_gather x1, blocking collectives, in_one_piece(): lax.all_gather(both, axis, axis=dim, tiled=True)  286 us
    gather x8, local copies, waits for them, and re-layouts, extrapolate(): chosen = jnp.take(pool_level, block_level, axis=1)  65.3 us
    dot_general x8, matrix products, extrapolate(): jnp.einsum('fsarkt,frktc->rfsac', picked, chosen, preferred_element_type=...  64.4 us
    ppermute x8, starting transfers between devices, extended_2(): lax.ppermute(lax.slice_in_dim(block, 0, width, axis=dim), axis, backward)  59.7 us
    gather x8, local copies, waits for them, and re-layouts, extrapolate(): jnp.take(tile_grid, local_ids, axis=3)  19.3 us
    ppermute x8, starting transfers between devices, extended_2(): lax.ppermute(lax.slice_in_dim(block, block.shape[dim] - width, None, axis...  15.4 us
    all_to_all x1, blocking collectives, copy_for_each(): return lax.all_to_all(copies, axis, split_axis=0, concat_axis=0, tiled=True)  14.3 us
    psum x1, blocking collectives, per_device(): summed = lax.psum(image_local, 'freq')  14.2 us
  transfers between devices with their start and end apart: 17, of which 0 were waited for; matrix products, arithmetic and copies ran while one was open for 17% of the time, Pallas kernels for 0%

profile of v1, /device:TPU:1, one launch (start us, length us, event | category | flops | bytes accessed | tf_op | source)
XLA Modules:
  0.0 629.9 jit_solution(18368570831199511457)
XLA Ops:
  0.8 14.3 %all_to_all.15 = f32[8,1,1024]{2,1,0:T(1,128)S(1)} all-to-all(f32[8,1,1024]{2,1,0:T(1,128)S(1)} %broadcast_in_dim.88), channel_id=1, replica_groups=mesh['depth'=8,'lat'=32,'freq'=2] {'depth'}, dimensions={0} | all-to-all | bytes 65536 | tf_op jit(solution)/shard_map/all_to_all | solution.py:37
  15.2 7.5 %stack.27 = bf16[8,1,3,8,128,256]{5,4,3,2,1,0:T(8,128)(2,1)} broadcast(bf16[3,8,128,256]{3,2,1,0:T(8,128)(2,1)} %bitcast.102), dimensions={2,3,4,5} | broadcast | bytes 14155776 | tf_op jit(solution)/shard_map/stack | solution.py:98
  28.3 285.6 %all_gather.3 = s32[8,8,21]{2,1,0:T(8,128)S(1)} all-gather(s32[1,8,21]{2,1,0:T(8,128)S(1)} %pad_add_fusion), channel_id=1, replica_groups=mesh['depth'=8,'lat'=32,'freq'=2] {'depth'}, dimensions={0}, use_global_device_ids=true | all-gather | bytes 6048 | tf_op jit(solution)/shard_map/all_gather | solution.py:27
  315.5 287.0 %while.17 = (s32[]{:T(128)}, bf16[3,2,16,1024]{3,2,1,0:T(8,128)(2,1)S(1)}, f32[8,1024]{1,0:T(8,128)}, s32[8,8,10]{2,1,0:T(8,128)S(1)}, s32[]{:T(128)}, /*index=5...) while((s32[]{:T(128)}, ...), condition=%wide.region_2.3_spmd, body=%wide.region_0.2_spmd.sunk | while | flops 515904960 | bytes 62015692 | solution.py:119
  315.5 12.9 %collective-permute-start = (bf16[3,2,16,1024]{3,2,1,0:T(8,128)(2,1)S(1)}, bf16[3,2,16,1024]{3,2,1,0:T(8,128)(2,1)S(1)}, u32[]{:S(2)}, u32[]{:S(2)}) collective-permute-start(bf16[3,2,16,1024]{3,2,1,0:T(8,128)(2,1)S(1)} %get-tuple-element.365), channel_id=1, source_target_pairs={{2,0},{4,2},{6,4},{8,6},{10,8},{12,10},{14,12},{16,14},{18,16},{20... | collective-permute-start | bytes 589832 | tf_op jit(solution)/shard_map/while/body/eval_jaxpr/ppermute | solution.py:19
  334.7 8.1 %gather_fusion = bf16[80,3,128,256]{3,2,1,0:T(8,128)(2,1)} fusion(bf16[3,8,128,256]{3,2,1,0:T(8,128)(2,1)S(1)} %dynamic-slice_bitcast_fusion.2, s32[1024]{0:T(1024)S(1)} %pad_clamp_fusion.4), kind=kCustom, calls=%fused_computation.1.clone.1 | custom fusion | bytes 31457600 | tf_op jit(solution)/shard_map/while/body/eval_jaxpr/jit(_take)/gather | solution.py:74
  347.0 8.0 %fusion.30 = f32[8,3,2,16,256]{4,3,2,1,0:T(8,128)S(1)} fusion(bf16[8,10,3,128,256]{4,3,2,1,0:T(8,128)(2,1)} %bitcast.100, pred[8,10]{1,0:T(8,128)(4,1)S(1)} %copy-done.5, bf16[8,10,3,2,16,128]{5,4,3,2,1,0:T(8,128)(2,1)} %bitcast.101, pred[8,10]{1,0:T(8,128)(4,1)S(1)} %copy-done.6, bf16[8,10]{1,0:T(8,128)(2,1)S(1)} %fusion.29), kind=kOutput, calls=%fused_computation.8.clone.1 | convolution fusion | flops 513146880 | bytes 18481472 | tf_op jit(solution)/shard_map/while/body/eval_jaxpr/fsarkt,frktc->rfsac/dot_general | solution.py:75
  369.8 8.2 %gather_fusion = bf16[80,3,128,256]{3,2,1,0:T(8,128)(2,1)} fusion(bf16[3,8,128,256]{3,2,1,0:T(8,128)(2,1)S(1)} %dynamic-slice_bitcast_fusion.2, s32[1024]{0:T(1024)S(1)} %pad_clamp_fusion.4), kind=kCustom, calls=%fused_computation.1.clone.1 | custom fusion | bytes 31457600 | tf_op jit(solution)/shard_map/while/body/eval_jaxpr/jit(_take)/gather | solution.py:74
  382.1 8.0 %fusion.30 = f32[8,3,2,16,256]{4,3,2,1,0:T(8,128)S(1)} fusion(bf16[8,10,3,128,256]{4,3,2,1,0:T(8,128)(2,1)} %bitcast.100, pred[8,10]{1,0:T(8,128)(4,1)S(1)} %copy-done.5, bf16[8,10,3,2,16,128]{5,4,3,2,1,0:T(8,128)(2,1)} %bitcast.101, pred[8,10]{1,0:T(8,128)(4,1)S(1)} %copy-done.6, bf16[8,10]{1,0:T(8,128)(2,1)S(1)} %fusion.29), kind=kOutput, calls=%fused_computation.8.clone.1 | convolution fusion | flops 513146880 | bytes 18481472 | tf_op jit(solution)/shard_map/while/body/eval_jaxpr/fsarkt,frktc->rfsac/dot_general | solution.py:75
  404.9 8.1 %gather_fusion = bf16[80,3,128,256]{3,2,1,0:T(8,128)(2,1)} fusion(bf16[3,8,128,256]{3,2,1,0:T(8,128)(2,1)S(1)} %dynamic-slice_bitcast_fusion.2, s32[1024]{0:T(1024)S(1)} %pad_clamp_fusion.4), kind=kCustom, calls=%fused_computation.1.clone.1 | custom fusion | bytes 31457600 | tf_op jit(solution)/shard_map/while/body/eval_jaxpr/jit(_take)/gather | solution.py:74
  417.2 8.0 %fusion.30 = f32[8,3,2,16,256]{4,3,2,1,0:T(8,128)S(1)} fusion(bf16[8,10,3,128,256]{4,3,2,1,0:T(8,128)(2,1)} %bitcast.100, pred[8,10]{1,0:T(8,128)(4,1)S(1)} %copy-done.5, bf16[8,10,3,2,16,128]{5,4,3,2,1,0:T(8,128)(2,1)} %bitcast.101, pred[8,10]{1,0:T(8,128)(4,1)S(1)} %copy-done.6, bf16[8,10]{1,0:T(8,128)(2,1)S(1)} %fusion.29), kind=kOutput, calls=%fused_computation.8.clone.1 | convolution fusion | flops 513146880 | bytes 18481472 | tf_op jit(solution)/shard_map/while/body/eval_jaxpr/fsarkt,frktc->rfsac/dot_general | solution.py:75
  427.0 6.7 %collective-permute-start = (bf16[3,2,16,1024]{3,2,1,0:T(8,128)(2,1)S(1)}, bf16[3,2,16,1024]{3,2,1,0:T(8,128)(2,1)S(1)}, u32[]{:S(2)}, u32[]{:S(2)}) collective-permute-start(bf16[3,2,16,1024]{3,2,1,0:T(8,128)(2,1)S(1)} %get-tuple-element.365), channel_id=1, source_target_pairs={{2,0},{4,2},{6,4},{8,6},{10,8},{12,10},{14,12},{16,14},{18,16},{20... | collective-permute-start | bytes 589832 | tf_op jit(solution)/shard_map/while/body/eval_jaxpr/ppermute | solution.py:19
  440.0 8.2 %gather_fusion = bf16[80,3,128,256]{3,2,1,0:T(8,128)(2,1)} fusion(bf16[3,8,128,256]{3,2,1,0:T(8,128)(2,1)S(1)} %dynamic-slice_bitcast_fusion.2, s32[1024]{0:T(1024)S(1)} %pad_clamp_fusion.4), kind=kCustom, calls=%fused_computation.1.clone.1 | custom fusion | bytes 31457600 | tf_op jit(solution)/shard_map/while/body/eval_jaxpr/jit(_take)/gather | solution.py:74
  452.4 8.0 %fusion.30 = f32[8,3,2,16,256]{4,3,2,1,0:T(8,128)S(1)} fusion(bf16[8,10,3,128,256]{4,3,2,1,0:T(8,128)(2,1)} %bitcast.100, pred[8,10]{1,0:T(8,128)(4,1)S(1)} %copy-done.5, bf16[8,10,3,2,16,128]{5,4,3,2,1,0:T(8,128)(2,1)} %bitcast.101, pred[8,10]{1,0:T(8,128)(4,1)S(1)} %copy-done.6, bf16[8,10]{1,0:T(8,128)(2,1)S(1)} %fusion.29), kind=kOutput, calls=%fused_computation.8.clone.1 | convolution fusion | flops 513146880 | bytes 18481472 | tf_op jit(solution)/shard_map/while/body/eval_jaxpr/fsarkt,frktc->rfsac/dot_general | solution.py:75
  475.1 8.1 %gather_fusion = bf16[80,3,128,256]{3,2,1,0:T(8,128)(2,1)} fusion(bf16[3,8,128,256]{3,2,1,0:T(8,128)(2,1)S(1)} %dynamic-slice_bitcast_fusion.2, s32[1024]{0:T(1024)S(1)} %pad_clamp_fusion.4), kind=kCustom, calls=%fused_computation.1.clone.1 | custom fusion | bytes 31457600 | tf_op jit(solution)/shard_map/while/body/eval_jaxpr/jit(_take)/gather | solution.py:74
  487.5 8.0 %fusion.30 = f32[8,3,2,16,256]{4,3,2,1,0:T(8,128)S(1)} fusion(bf16[8,10,3,128,256]{4,3,2,1,0:T(8,128)(2,1)} %bitcast.100, pred[8,10]{1,0:T(8,128)(4,1)S(1)} %copy-done.5, bf16[8,10,3,2,16,128]{5,4,3,2,1,0:T(8,128)(2,1)} %bitcast.101, pred[8,10]{1,0:T(8,128)(4,1)S(1)} %copy-done.6, bf16[8,10]{1,0:T(8,128)(2,1)S(1)} %fusion.29), kind=kOutput, calls=%fused_computation.8.clone.1 | convolution fusion | flops 513146880 | bytes 18481472 | tf_op jit(solution)/shard_map/while/body/eval_jaxpr/fsarkt,frktc->rfsac/dot_general | solution.py:75
  510.3 8.2 %gather_fusion = bf16[80,3,128,256]{3,2,1,0:T(8,128)(2,1)} fusion(bf16[3,8,128,256]{3,2,1,0:T(8,128)(2,1)S(1)} %dynamic-slice_bitcast_fusion.2, s32[1024]{0:T(1024)S(1)} %pad_clamp_fusion.4), kind=kCustom, calls=%fused_computation.1.clone.1 | custom fusion | bytes 31457600 | tf_op jit(solution)/shard_map/while/body/eval_jaxpr/jit(_take)/gather | solution.py:74
  522.6 8.0 %fusion.30 = f32[8,3,2,16,256]{4,3,2,1,0:T(8,128)S(1)} fusion(bf16[8,10,3,128,256]{4,3,2,1,0:T(8,128)(2,1)} %bitcast.100, pred[8,10]{1,0:T(8,128)(4,1)S(1)} %copy-done.5, bf16[8,10,3,2,16,128]{5,4,3,2,1,0:T(8,128)(2,1)} %bitcast.101, pred[8,10]{1,0:T(8,128)(4,1)S(1)} %copy-done.6, bf16[8,10]{1,0:T(8,128)(2,1)S(1)} %fusion.29), kind=kOutput, calls=%fused_computation.8.clone.1 | convolution fusion | flops 513146880 | bytes 18481472 | tf_op jit(solution)/shard_map/while/body/eval_jaxpr/fsarkt,frktc->rfsac/dot_general | solution.py:75
  545.3 8.2 %gather_fusion = bf16[80,3,128,256]{3,2,1,0:T(8,128)(2,1)} fusion(bf16[3,8,128,256]{3,2,1,0:T(8,128)(2,1)S(1)} %dynamic-slice_bitcast_fusion.2, s32[1024]{0:T(1024)S(1)} %pad_clamp_fusion.4), kind=kCustom, calls=%fused_computation.1.clone.1 | custom fusion | bytes 31457600 | tf_op jit(solution)/shard_map/while/body/eval_jaxpr/jit(_take)/gather | solution.py:74
  557.7 8.0 %fusion.30 = f32[8,3,2,16,256]{4,3,2,1,0:T(8,128)S(1)} fusion(bf16[8,10,3,128,256]{4,3,2,1,0:T(8,128)(2,1)} %bitcast.100, pred[8,10]{1,0:T(8,128)(4,1)S(1)} %copy-done.5, bf16[8,10,3,2,16,128]{5,4,3,2,1,0:T(8,128)(2,1)} %bitcast.101, pred[8,10]{1,0:T(8,128)(4,1)S(1)} %copy-done.6, bf16[8,10]{1,0:T(8,128)(2,1)S(1)} %fusion.29), kind=kOutput, calls=%fused_computation.8.clone.1 | convolution fusion | flops 513146880 | bytes 18481472 | tf_op jit(solution)/shard_map/while/body/eval_jaxpr/fsarkt,frktc->rfsac/dot_general | solution.py:75
  580.4 8.2 %gather_fusion = bf16[80,3,128,256]{3,2,1,0:T(8,128)(2,1)} fusion(bf16[3,8,128,256]{3,2,1,0:T(8,128)(2,1)S(1)} %dynamic-slice_bitcast_fusion.2, s32[1024]{0:T(1024)S(1)} %pad_clamp_fusion.4), kind=kCustom, calls=%fused_computation.1.clone.1 | custom fusion | bytes 31457600 | tf_op jit(solution)/shard_map/while/body/eval_jaxpr/jit(_take)/gather | solution.py:74
  592.8 8.0 %fusion.30 = f32[8,3,2,16,256]{4,3,2,1,0:T(8,128)S(1)} fusion(bf16[8,10,3,128,256]{4,3,2,1,0:T(8,128)(2,1)} %bitcast.100, pred[8,10]{1,0:T(8,128)(4,1)S(1)} %copy-done.5, bf16[8,10,3,2,16,128]{5,4,3,2,1,0:T(8,128)(2,1)} %bitcast.101, pred[8,10]{1,0:T(8,128)(4,1)S(1)} %copy-done.6, bf16[8,10]{1,0:T(8,128)(2,1)S(1)} %fusion.29), kind=kOutput, calls=%fused_computation.8.clone.1 | convolution fusion | flops 513146880 | bytes 18481472 | tf_op jit(solution)/shard_map/while/body/eval_jaxpr/fsarkt,frktc->rfsac/dot_general | solution.py:75
  603.3 11.7 %all_to_all.16 = f32[8,1,1024]{2,1,0:T(1,128)S(1)} all-to-all(f32[8,1,1024]{2,1,0:T(1,128)S(1)} %reshape.225), channel_id=1, replica_groups=mesh['depth'=8,'lat'=32,'freq'=2] {'depth'}, dimensions={0} | all-to-all | bytes 65536 | tf_op jit(solution)/shard_map/all_to_all | solution.py:58
  615.1 14.2 %psum.7 = f32[1024]{0:T(1024)S(1)} all-reduce(f32[1024]{0:T(1024)S(1)} %reduce_sum.20), channel_id=1, replica_groups=mesh['depth'=8,'lat'=32,'freq'=2] {'freq'}, use_global_device_ids=true, to_apply=%region_4.5 | all-reduce | flops 1024 | bytes 8192 | tf_op jit(solution)/shard_map/psum | solution.py:121
  (276 shorter events, 146.3 us)
Async XLA Ops:
  0.0 314.8 %copy-start = (bf16[3,2,128,1024]{3,2,1,0:T(8,128)(2,1)S(1)}, bf16[3,2,128,1024]{3,2,1,0:T(8,128)(2,1)}, u32[]{:S(2)}) copy-start(bf16[3,2,128,1024]{3,2,1,0:T(8,128)(2,1)} %param.8) | copy-start | bytes 4718596
  22.7 292.8 %all-to-all-start = ((bf16[8,1,3,8,128,256]{5,4,3,2,1,0:T(8,128)(2,1)}), bf16[8,1,3,8,128,256]{5,4,3,2,1,0:T(8,128)(2,1)}, u32[]{:S(2)}, u32[]{:S(2)}) async-start(bf16[8,1,3,8,128,256]{5,4,3,2,1,0:T(8,128)(2,1)} %stack.27), calls=%async_computation | async-start | bytes 25165824 | tf_op jit(solution)/shard_map/all_to_all | solution.py:98
  315.5 15.6 %copy-start.1 = (s32[8,8,10]{2,1,0:T(8,128)}, s32[8,8,10]{2,1,0:T(8,128)S(1)}, u32[]{:S(2)}) copy-start(s32[8,8,10]{2,1,0:T(8,128)S(1)} %get-tuple-element.381) | copy-start | bytes 7684 | tf_op jit(solution)/shard_map/while
  315.5 15.6 %copy-start.3 = (s32[8,8,10]{2,1,0:T(8,128)}, s32[8,8,10]{2,1,0:T(8,128)S(1)}, u32[]{:S(2)}) copy-start(s32[8,8,10]{2,1,0:T(8,128)S(1)} %get-tuple-element.378) | copy-start | bytes 7684 | tf_op jit(solution)/shard_map/while
  315.5 28.0 %collective-permute-start = (bf16[3,2,16,1024]{3,2,1,0:T(8,128)(2,1)S(1)}, bf16[3,2,16,1024]{3,2,1,0:T(8,128)(2,1)S(1)}, u32[]{:S(2)}, u32[]{:S(2)}) collective-permute-start(bf16[3,2,16,1024]{3,2,1,0:T(8,128)(2,1)S(1)} %get-tuple-element.365), channel_id=1, source_target_pairs={{2,0},{4,2},{6,4},{8,6},{10,8},{12,10},{14,12},{16,14},{18,16},{20... | collective-permute-start | bytes 589832 | tf_op jit(solution)/shard_map/while/body/eval_jaxpr/ppermute | solution.py:19
  328.4 15.1 %collective-permute-start.1 = (bf16[3,2,16,1024]{3,2,1,0:T(8,128)(2,1)S(1)}, bf16[3,2,16,1024]{3,2,1,0:T(8,128)(2,1)}, u32[]{:S(2)}, u32[]{:S(2)}) collective-permute-start(bf16[3,2,16,1024]{3,2,1,0:T(8,128)(2,1)S(1)} %get-tuple-element.365), channel_id=1, source_target_pairs={{0,2},{2,4},{4,6},{6,8},{8,10},{10,12},{12,14},{14,16},{16,18},{18... | collective-permute-start | bytes 589832 | tf_op jit(solution)/shard_map/while/body/eval_jaxpr/ppermute | solution.py:16
  356.8 9.4 %copy-start.3 = (s32[8,8,10]{2,1,0:T(8,128)}, s32[8,8,10]{2,1,0:T(8,128)S(1)}, u32[]{:S(2)}) copy-start(s32[8,8,10]{2,1,0:T(8,128)S(1)} %get-tuple-element.378) | copy-start | bytes 7684 | tf_op jit(solution)/shard_map/while
  356.8 21.9 %collective-permute-start = (bf16[3,2,16,1024]{3,2,1,0:T(8,128)(2,1)S(1)}, bf16[3,2,16,1024]{3,2,1,0:T(8,128)(2,1)S(1)}, u32[]{:S(2)}, u32[]{:S(2)}) collective-permute-start(bf16[3,2,16,1024]{3,2,1,0:T(8,128)(2,1)S(1)} %get-tuple-element.365), channel_id=1, source_target_pairs={{2,0},{4,2},{6,4},{8,6},{10,8},{12,10},{14,12},{16,14},{18,16},{20... | collective-permute-start | bytes 589832 | tf_op jit(solution)/shard_map/while/body/eval_jaxpr/ppermute | solution.py:19
  363.5 15.2 %collective-permute-start.1 = (bf16[3,2,16,1024]{3,2,1,0:T(8,128)(2,1)S(1)}, bf16[3,2,16,1024]{3,2,1,0:T(8,128)(2,1)}, u32[]{:S(2)}, u32[]{:S(2)}) collective-permute-start(bf16[3,2,16,1024]{3,2,1,0:T(8,128)(2,1)S(1)} %get-tuple-element.365), channel_id=1, source_target_pairs={{0,2},{2,4},{4,6},{6,8},{8,10},{10,12},{12,14},{14,16},{16,18},{18... | collective-permute-start | bytes 589832 | tf_op jit(solution)/shard_map/while/body/eval_jaxpr/ppermute | solution.py:16
  391.9 21.8 %collective-permute-start = (bf16[3,2,16,1024]{3,2,1,0:T(8,128)(2,1)S(1)}, bf16[3,2,16,1024]{3,2,1,0:T(8,128)(2,1)S(1)}, u32[]{:S(2)}, u32[]{:S(2)}) collective-permute-start(bf16[3,2,16,1024]{3,2,1,0:T(8,128)(2,1)S(1)} %get-tuple-element.365), channel_id=1, source_target_pairs={{2,0},{4,2},{6,4},{8,6},{10,8},{12,10},{14,12},{16,14},{18,16},{20... | collective-permute-start | bytes 589832 | tf_op jit(solution)/shard_map/while/body/eval_jaxpr/ppermute | solution.py:19
  398.6 15.1 %collective-permute-start.1 = (bf16[3,2,16,1024]{3,2,1,0:T(8,128)(2,1)S(1)}, bf16[3,2,16,1024]{3,2,1,0:T(8,128)(2,1)}, u32[]{:S(2)}, u32[]{:S(2)}) collective-permute-start(bf16[3,2,16,1024]{3,2,1,0:T(8,128)(2,1)S(1)} %get-tuple-element.365), channel_id=1, source_target_pairs={{0,2},{2,4},{4,6},{6,8},{8,10},{10,12},{12,14},{14,16},{16,18},{18... | collective-permute-start | bytes 589832 | tf_op jit(solution)/shard_map/while/body/eval_jaxpr/ppermute | solution.py:16
  427.0 9.4 %copy-start.1 = (s32[8,8,10]{2,1,0:T(8,128)}, s32[8,8,10]{2,1,0:T(8,128)S(1)}, u32[]{:S(2)}) copy-start(s32[8,8,10]{2,1,0:T(8,128)S(1)} %get-tuple-element.381) | copy-start | bytes 7684 | tf_op jit(solution)/shard_map/while
  427.0 9.4 %copy-start.3 = (s32[8,8,10]{2,1,0:T(8,128)}, s32[8,8,10]{2,1,0:T(8,128)S(1)}, u32[]{:S(2)}) copy-start(s32[8,8,10]{2,1,0:T(8,128)S(1)} %get-tuple-element.378) | copy-start | bytes 7684 | tf_op jit(solution)/shard_map/while
  427.0 21.9 %collective-permute-start = (bf16[3,2,16,1024]{3,2,1,0:T(8,128)(2,1)S(1)}, bf16[3,2,16,1024]{3,2,1,0:T(8,128)(2,1)S(1)}, u32[]{:S(2)}, u32[]{:S(2)}) collective-permute-start(bf16[3,2,16,1024]{3,2,1,0:T(8,128)(2,1)S(1)} %get-tuple-element.365), channel_id=1, source_target_pairs={{2,0},{4,2},{6,4},{8,6},{10,8},{12,10},{14,12},{16,14},{18,16},{20... | collective-permute-start | bytes 589832 | tf_op jit(solution)/shard_map/while/body/eval_jaxpr/ppermute | solution.py:19
  433.7 15.2 %collective-permute-start.1 = (bf16[3,2,16,1024]{3,2,1,0:T(8,128)(2,1)S(1)}, bf16[3,2,16,1024]{3,2,1,0:T(8,128)(2,1)}, u32[]{:S(2)}, u32[]{:S(2)}) collective-permute-start(bf16[3,2,16,1024]{3,2,1,0:T(8,128)(2,1)S(1)} %get-tuple-element.365), channel_id=1, source_target_pairs={{0,2},{2,4},{4,6},{6,8},{8,10},{10,12},{12,14},{14,16},{16,18},{18... | collective-permute-start | bytes 589832 | tf_op jit(solution)/shard_map/while/body/eval_jaxpr/ppermute | solution.py:16
  462.2 21.8 %collective-permute-start = (bf16[3,2,16,1024]{3,2,1,0:T(8,128)(2,1)S(1)}, bf16[3,2,16,1024]{3,2,1,0:T(8,128)(2,1)S(1)}, u32[]{:S(2)}, u32[]{:S(2)}) collective-permute-start(bf16[3,2,16,1024]{3,2,1,0:T(8,128)(2,1)S(1)} %get-tuple-element.365), channel_id=1, source_target_pairs={{2,0},{4,2},{6,4},{8,6},{10,8},{12,10},{14,12},{16,14},{18,16},{20... | collective-permute-start | bytes 589832 | tf_op jit(solution)/shard_map/while/body/eval_jaxpr/ppermute | solution.py:19
  468.9 15.1 %collective-permute-start.1 = (bf16[3,2,16,1024]{3,2,1,0:T(8,128)(2,1)S(1)}, bf16[3,2,16,1024]{3,2,1,0:T(8,128)(2,1)}, u32[]{:S(2)}, u32[]{:S(2)}) collective-permute-start(bf16[3,2,16,1024]{3,2,1,0:T(8,128)(2,1)S(1)} %get-tuple-element.365), channel_id=1, source_target_pairs={{0,2},{2,4},{4,6},{6,8},{8,10},{10,12},{12,14},{14,16},{16,18},{18... | collective-permute-start | bytes 589832 | tf_op jit(solution)/shard_map/while/body/eval_jaxpr/ppermute | solution.py:16
  497.2 9.4 %copy-start.3 = (s32[8,8,10]{2,1,0:T(8,128)}, s32[8,8,10]{2,1,0:T(8,128)S(1)}, u32[]{:S(2)}) copy-start(s32[8,8,10]{2,1,0:T(8,128)S(1)} %get-tuple-element.378) | copy-start | bytes 7684 | tf_op jit(solution)/shard_map/while
  497.2 21.9 %collective-permute-start = (bf16[3,2,16,1024]{3,2,1,0:T(8,128)(2,1)S(1)}, bf16[3,2,16,1024]{3,2,1,0:T(8,128)(2,1)S(1)}, u32[]{:S(2)}, u32[]{:S(2)}) collective-permute-start(bf16[3,2,16,1024]{3,2,1,0:T(8,128)(2,1)S(1)} %get-tuple-element.365), channel_id=1, source_target_pairs={{2,0},{4,2},{6,4},{8,6},{10,8},{12,10},{14,12},{16,14},{18,16},{20... | collective-permute-start | bytes 589832 | tf_op jit(solution)/shard_map/while/body/eval_jaxpr/ppermute | solution.py:19
  504.0 15.2 %collective-permute-start.1 = (bf16[3,2,16,1024]{3,2,1,0:T(8,128)(2,1)S(1)}, bf16[3,2,16,1024]{3,2,1,0:T(8,128)(2,1)}, u32[]{:S(2)}, u32[]{:S(2)}) collective-permute-start(bf16[3,2,16,1024]{3,2,1,0:T(8,128)(2,1)S(1)} %get-tuple-element.365), channel_id=1, source_target_pairs={{0,2},{2,4},{4,6},{6,8},{8,10},{10,12},{12,14},{14,16},{16,18},{18... | collective-permute-start | bytes 589832 | tf_op jit(solution)/shard_map/while/body/eval_jaxpr/ppermute | solution.py:16
  532.4 21.8 %collective-permute-start = (bf16[3,2,16,1024]{3,2,1,0:T(8,128)(2,1)S(1)}, bf16[3,2,16,1024]{3,2,1,0:T(8,128)(2,1)S(1)}, u32[]{:S(2)}, u32[]{:S(2)}) collective-permute-start(bf16[3,2,16,1024]{3,2,1,0:T(8,128)(2,1)S(1)} %get-tuple-element.365), channel_id=1, source_target_pairs={{2,0},{4,2},{6,4},{8,6},{10,8},{12,10},{14,12},{16,14},{18,16},{20... | collective-permute-start | bytes 589832 | tf_op jit(solution)/shard_map/while/body/eval_jaxpr/ppermute | solution.py:19
  539.0 15.2 %collective-permute-start.1 = (bf16[3,2,16,1024]{3,2,1,0:T(8,128)(2,1)S(1)}, bf16[3,2,16,1024]{3,2,1,0:T(8,128)(2,1)}, u32[]{:S(2)}, u32[]{:S(2)}) collective-permute-start(bf16[3,2,16,1024]{3,2,1,0:T(8,128)(2,1)S(1)} %get-tuple-element.365), channel_id=1, source_target_pairs={{0,2},{2,4},{4,6},{6,8},{8,10},{10,12},{12,14},{14,16},{16,18},{18... | collective-permute-start | bytes 589832 | tf_op jit(solution)/shard_map/while/body/eval_jaxpr/ppermute | solution.py:16
  567.4 21.8 %collective-permute-start = (bf16[3,2,16,1024]{3,2,1,0:T(8,128)(2,1)S(1)}, bf16[3,2,16,1024]{3,2,1,0:T(8,128)(2,1)S(1)}, u32[]{:S(2)}, u32[]{:S(2)}) collective-permute-start(bf16[3,2,16,1024]{3,2,1,0:T(8,128)(2,1)S(1)} %get-tuple-element.365), channel_id=1, source_target_pairs={{2,0},{4,2},{6,4},{8,6},{10,8},{12,10},{14,12},{16,14},{18,16},{20... | collective-permute-start | bytes 589832 | tf_op jit(solution)/shard_map/while/body/eval_jaxpr/ppermute | solution.py:19
  574.1 15.1 %collective-permute-start.1 = (bf16[3,2,16,1024]{3,2,1,0:T(8,128)(2,1)S(1)}, bf16[3,2,16,1024]{3,2,1,0:T(8,128)(2,1)}, u32[]{:S(2)}, u32[]{:S(2)}) collective-permute-start(bf16[3,2,16,1024]{3,2,1,0:T(8,128)(2,1)S(1)} %get-tuple-element.365), channel_id=1, source_target_pairs={{0,2},{2,4},{4,6},{6,8},{8,10},{10,12},{12,14},{14,16},{16,18},{18... | collective-permute-start | bytes 589832 | tf_op jit(solution)/shard_map/while/body/eval_jaxpr/ppermute | solution.py:16
  (45 other events, 176.5 us)
